TPU v7x, 512 devices: a whole 4x8x8 slice. The times are simulated.
512 devices in a mesh: tok: 16 (over y_lo, x), voc: 32 (over y_hi, z, core).
Axes of the slice: x: 4, y: 8 (y_hi: 2, y_lo: 4; y = y_hi * 4 + y_lo), z: 8, core: 2. Of those that a mesh axis runs over, the one named last changes fastest.
Arguments:
- hidden: bfloat16 [8192, 1024], P('tok', 'voc'), may hold values from -6 to 6
- weight_values: bfloat16 [1024, 131072], P('tok', 'voc'), may hold values from -0.1875 to 0.1875
- scales: float32 [1024, 1024], P('tok', 'voc'), may hold values from 0.25 to 4
- partial_logits: bfloat16 [8192, 131072], P('tok', 'voc'), may hold values from -56 to 402
- targets: int32 [8192], P('tok'), may hold values from 0 to 131071
Outputs:
- loss: float32 [8192], P('tok')
All inputs are finite; a program needn't handle non-finite values.
Results may differ from a plain program's by a relative error of at most 0.0015.
Values may be sent and summed in bfloat16 or wider, within the bound.
A program may use at most 128 MiB of HBM per device.

v0:
```python
import jax
import jax.numpy as jnp
from jax import lax
from jax.sharding import PartitionSpec as P


def expand(values, block_scales):
    count, width = values.shape
    groups = block_scales.shape[1]
    scaled = (
        values.astype(jnp.float32).reshape(count, groups, width // groups)
        * block_scales[:, :, None]
    )
    return scaled.reshape(count, width).astype(jnp.bfloat16)


def on_device(hidden, weight_values, scales, partial_logits, targets):
    width = weight_values.shape[1]
    wide = lax.all_gather(hidden, "voc", axis=1, tiled=True)
    window = jnp.dot(
        wide,
        expand(
            lax.all_gather(weight_values, "tok", axis=0, tiled=True),
            lax.all_gather(scales.astype(jnp.bfloat16), "tok", axis=0, tiled=True).astype(
                jnp.float32
            ),
        ),
        preferred_element_type=jnp.float32,
    )
    full = partial_logits.astype(jnp.float32) + window
    column_ids = lax.axis_index("voc") * width + lax.iota(jnp.int32, width)
    local_pick = jnp.sum(jnp.where(column_ids[None, :] == targets[:, None], full, 0.0), axis=1)
    local_top = jnp.max(full, axis=1)
    top = lax.pmax(local_top, "voc")
    total, picked = lax.psum((jnp.sum(jnp.exp(full - top[:, None]), axis=1), local_pick), "voc")
    return top + jnp.log(total) - picked


def solution(mesh):
    in_specs = (P("tok", "voc"), P("tok", "voc"), P("tok", "voc"), P("tok", "voc"), P("tok"))
    out_specs = P("tok")
    return jax.shard_map(
        on_device, mesh=mesh, in_specs=in_specs, out_specs=out_specs, check_vma=False
    )
```

profile of v0, /device:TPU:1, one launch (start us, length us, event | category | flops | bytes accessed | tf_op | source)
XLA Modules:
  0.0 433.9 jit_solution(6033054006162960983)
XLA Ops:
  6.5 0.0 all-gather.6.cloned.1.call-start
  6.5 0.7 all-gather.6.cloned.1.call-update
  7.3 0.0 all-gather.4.cloned.1.call-start
  7.3 0.7 all-gather.4.cloned.1.call-update
  8.0 0.7 convert_bitcast_fusion
  8.7 37.1 %all-gather = bf16[16,64,32]{1,2,0:T(8,128)(2,1)S(1)} all-gather(bf16[1,64,32]{1,2,0:T(8,128)(2,1)S(1)} %convert_bitcast_fusion), channel_id=1, replica_groups=mesh['tok'=16,'voc'=32] {'tok'}, dimensions={0}, use_global_device_ids=true | all-gather | bytes 69632 | tf_op jit(solution)/shard_map/all_gather | solution.py:24
  45.8 0.1 copy.13
  46.0 6.5 %copy.10 = bf16[512,4096]{0,1:T(8,128)(2,1)} copy(bf16[512,4096]{1,0:T(8,128)(2,1)} %param.8) | data formatting | bytes 8388608 | tf_op args[3]
  52.5 49.9 %all-gather.6.cloned.1.call-done = bf16[512,1024]{0,1:T(8,128)(2,1)} async-done(((bf16[512,32]{0,1:T(8,128)(2,1)}), bf16[512,1024]{0,1:T(8,128)(2,1)}) %all-gather.6.cloned.1.call-update) | async-done | bytes 1048592 | tf_op jit(solution)/shard_map/all_gather | solution.py:19
  102.3 102.5 %all-gather.4.cloned.1.call-done = bf16[1024,4096]{1,0:T(8,128)(2,1)} async-done(((bf16[64,4096]{1,0:T(8,128)(2,1)}), bf16[1024,4096]{1,0:T(8,128)(2,1)}) %all-gather.4.cloned.1.call-update) | async-done | bytes 8388624 | tf_op jit(solution)/shard_map/all_gather | solution.py:23
  204.9 0.0 copy-start
  204.9 0.0 copy-start.1
  204.9 11.1 %mul.14 = f32[1024,32,128]{2,1,0:T(8,128)} broadcast(f32[1024,32]{1,0:T(8,128)S(1)} %bitcast.17), dimensions={0,1} | broadcast | bytes 16908288 | tf_op jit(solution)/shard_map/mul | solution.py:11
  216.0 0.0 copy-done
  216.0 0.0 copy-done.1
  216.0 0.0 copy-start.2
  216.0 31.2 %fusion.5 = (f32[512]{0:T(512)S(1)}, f32[512,4096]{0,1:T(8,128)}) fusion(bf16[512,1024]{0,1:T(8,128)(2,1)S(1)} %copy-done.1, f32[128,8,32,128]{3,2,1,0:T(8,128)} %bitcast.16, bf16[1024,4096]{1,0:T(8,128)(2,1)} %all-gather.4.cloned.1.call-done, bf16[512,4096]{0,1:T(8,128)(2,1)S(1)} %copy-done), kind=kOutput, calls=%fused_computation.9 | convolution fusion | flops 4313841152 | bytes 38799360 | tf_op jit(solution)/shard_map/dot_general | solution.py:20
  247.2 84.3 %pmax.7 = f32[512]{0:T(512)S(1)} all-reduce(f32[512]{0:T(512)S(1)} %get-tuple-element.9), channel_id=1, replica_groups=mesh['tok'=16,'voc'=32] {'voc'}, use_global_device_ids=true, to_apply=%region_1.2 | all-reduce | flops 512 | bytes 4096 | tf_op jit(solution)/shard_map/pmax | solution.py:34
  331.5 0.0 copy-done.2
  331.5 5.2 %exponential_reduce_fusion = (f32[512]{0:T(512)S(1)}, f32[512]{0:T(512)S(1)}) fusion(f32[512,4096]{0,1:T(8,128)} %get-tuple-element.10, f32[512]{0:T(512)S(1)} %pmax.7, s32[512]{0:T(512)S(1)} %copy-done.2, s32[4096]{0:T(1024)S(1)} %iota_add_fusion), kind=kLoop, calls=%fused_computation.5 | loop fusion | flops 10484736 | bytes 8413184 | tf_op jit(solution)/shard_map/reduce_sum | solution.py:35
  336.6 89.8 %all-reduce = (f32[512]{0:T(512)S(1)}, f32[512]{0:T(512)S(1)}) all-reduce(f32[512]{0:T(512)S(1)} %get-tuple-element.6, f32[512]{0:T(512)S(1)} %get-tuple-element.5), channel_id=1, replica_groups=mesh['tok'=16,'voc'=32] {'voc'}, use_global_device_ids=true, to_apply=%region_5.6 | all-reduce | flops 1024 | bytes 8192 | tf_op jit(solution)/shard_map/psum | solution.py:35
  426.5 0.6 add_subtract_fusion
  (1 shorter events, 0.0 us)
Async XLA Ops:
  6.5 95.8 %all-gather.6.cloned.1.call-start = ((), (), s32[]{:S(2)}) async-start(), calls=%async_computation.1 | async-start | bytes 1081344 | tf_op jit(solution)/shard_map/all_gather | solution.py:19
  7.3 197.6 %all-gather.4.cloned.1.call-start = ((), (), s32[]{:S(2)}) async-start(), calls=%async_computation | async-start | bytes 8912896 | tf_op jit(solution)/shard_map/all_gather | solution.py:23
  204.9 11.1 %copy-start = (bf16[512,4096]{0,1:T(8,128)(2,1)S(1)}, bf16[512,4096]{0,1:T(8,128)(2,1)}, u32[]{:S(2)}) copy-start(bf16[512,4096]{0,1:T(8,128)(2,1)} %copy.10) | copy-start | bytes 12582916
  204.9 11.1 %copy-start.1 = (bf16[512,1024]{0,1:T(8,128)(2,1)S(1)}, bf16[512,1024]{0,1:T(8,128)(2,1)}, u32[]{:S(2)}) copy-start(bf16[512,1024]{0,1:T(8,128)(2,1)} %all-gather.6.cloned.1.call-done) | copy-start | bytes 3145732
  216.0 115.5 %copy-start.2 = (s32[512]{0:T(512)S(1)}, s32[512]{0:T(512)}, u32[]{:S(2)}) copy-start(s32[512]{0:T(512)} %param.9) | copy-start | bytes 6148
Sparse Core Ops, SparseCore 0:
  10.7 91.5 all-gather.5
  104.4 100.3 all-gather.3
where the time goes:
time: 434 us
  blocking collectives  211 us (49%)
  waiting for transfers between devices  154 us (35%)
  matrix products  31.2 us (7%)
  local copies, waits for them, and re-layouts  17.8 us (4%)
  between operations  13.4 us (3%)
  other arithmetic  6.47 us (1%)
    all_gather x1, waiting for transfers between devices, on_device(): lax.all_gather(weight_values, 'tok', axis=0, tiled=True)  103 us
    psum x1, blocking collectives, on_device(): lax.psum((jnp.sum(jnp.exp(full - top[:, None]), axis=1), local_pick), 'voc')  89.8 us
    pmax x1, blocking collectives, on_device(): top = lax.pmax(local_top, 'voc')  84.3 us
    all_gather x1, waiting for transfers between devices, on_device(): wide = lax.all_gather(hidden, 'voc', axis=1, tiled=True)  49.9 us
    all_gather x1, blocking collectives, on_device(): lax.all_gather(scales.astype(jnp.bfloat16), 'tok', axis=0, tiled=True)  37.1 us
    dot_general x1, matrix products, on_device(): jnp.dot(wide, expand(lax.all_gather(weight_values, 'tok', axis=0, tiled=T...  31.2 us
    mul x1, local copies, waits for them, and re-layouts, expand(): values.astype(jnp.float32).reshape(count, groups, width // groups)  11.1 us
  transfers between devices with their start and end apart: 2, of which 2 were waited for; matrix products, arithmetic and copies ran while one was open for 2% of the time, Pallas kernels for 0%

commit v1 on v0

v1 whole, which is shorter than its diff:
```python
import functools

import jax
import jax.numpy as jnp
from jax import lax
from jax.experimental import pallas as pl
from jax.experimental.pallas import tpu as pltpu
from jax.sharding import PartitionSpec as P

MESH = pl.DeviceIdType.MESH
NX, NY, NZ = 4, 4, 8
ROWS, KLOC, VLOC, KSH, SB = 512, 64, 4096, 32, 128
QG = 7
QA = QG * SB
BC = VLOC - 4 * QA
BG = BC // SB
RC = 256
NRC = ROWS // RC


def kernel(
    hid_ref, w_ref, sc_ref, part_ref, tgt_ref, out_ref,
    ws, wa, wb, ht, hh, pa, pb, tg, tt, st, stb, sx, sv, sz,
    hy_s, hy_r, hx_s, hx_r, z_s, z_r, c_s, c_r, wax_s, wax_r, wbx_s, wbx_r,
    ya_s, ya_r, yb_s, yb_r, pa_s, pa_r, pa_l, pb_l, tg_s, tg_r, sx_s, sx_r, sv_s, sv_r, sz_s, sz_r,
):
    t_id, v_id = lax.axis_index("tok"), lax.axis_index("voc")
    x, y = lax.rem(t_id, NX), lax.div(t_id, NX)
    yh, z, c = lax.div(v_id, 16), lax.rem(lax.div(v_id, 2), NZ), lax.rem(v_id, 2)

    def dev(x_=None, y_=None, yh_=None, z_=None, c_=None):
        x_, y_ = x if x_ is None else x_, y if y_ is None else y_
        yh_, z_, c_ = yh if yh_ is None else yh_, z if z_ is None else z_, c if c_ is None else c_
        return (y_ * NX + x_, yh_ * 16 + z_ * 2 + c_)

    def xp(r):
        return lax.rem(x + r, NX)

    def xm(r):
        return lax.rem(x + NX - r, NX)

    def copy(src, dst, ss, rs, to):
        return pltpu.make_async_remote_copy(
            src_ref=src, dst_ref=dst, send_sem=ss, recv_sem=rs, device_id=to, device_id_type=MESH
        )

    bar = pltpu.get_barrier_semaphore()

    def greet(to):
        pl.semaphore_signal(bar, inc=1, device_id=to, device_id_type=MESH)

    for r in range(1, NX):
        greet(dev(x_=xp(r)))
    for r in range(1, NZ):
        greet(dev(z_=lax.rem(z + r, NZ)))
    for r in range(1, 4):
        greet(dev(yh_=lax.rem(yh + r // 2, 2), c_=lax.rem(c + r % 2, 2)))

    @pl.when(y > 0)
    def _():
        greet(dev(y_=y - 1))

    @pl.when(y < NY - 1)
    def _():
        greet(dev(y_=y + 1))

    own_pa = [
        pltpu.make_async_copy(
            part_ref.at[pl.ds(i * RC, RC), pl.ds(pl.multiple_of(x * QA, SB), QA)],
            pa.at[x, pl.ds(i * RC, RC)], pa_l.at[i],
        )
        for i in range(NRC)
    ]
    for d in own_pa:
        d.start()
    own_pb = pltpu.make_async_copy(part_ref.at[:, pl.ds(4 * QA, BC)], pb, pb_l)
    own_pb.start()

    def dense(g):
        scaled = w_ref[:, g * SB:(g + 1) * SB].astype(jnp.float32) * sc_ref[:, g:g + 1]
        return scaled.astype(jnp.bfloat16)

    for q in range(NX):
        for g in range(QG):
            ws[q, :, g * SB:(g + 1) * SB] = dense(q * QG + g)
    for g in range(BG):
        wb[t_id, :, g * SB:(g + 1) * SB] = dense(4 * QG + g)
    wa[t_id] = ws[x]
    eye = (
        lax.broadcasted_iota(jnp.int32, (KSH, KSH), 0) == lax.broadcasted_iota(jnp.int32, (KSH, KSH), 1)
    ).astype(jnp.bfloat16)
    ht[x, yh, z, c] = lax.dot_general(
        eye, hid_ref[...], (((1,), (1,)), ((), ())), preferred_element_type=jnp.float32
    ).astype(jnp.bfloat16)
    tg[x] = tgt_ref[...]

    near = jnp.where(y > 0, 1, 0) + jnp.where(y < NY - 1, 1, 0)
    pl.semaphore_wait(bar, (NX - 1) + (NZ - 1) + 3 + near)

    sends = []

    def start(d):
        d.start()
        sends.append(d)

    hy = copy(ht.at[x, yh, z, c], ht.at[x, yh, z, c], hy_s, hy_r, dev(yh_=1 - yh))
    start(hy)

    def hx(stream, r):
        ref = ht.at[x, yh if stream == 0 else 1 - yh, z, c]
        return copy(ref, ref, hx_s.at[stream, r], hx_r.at[stream, r], dev(x_=xp(r)))

    def hx_wait(stream, r):
        ref = ht.at[xm(r), yh if stream == 0 else 1 - yh, z, c]
        copy(ref, ref, hx_s.at[stream, r], hx_r.at[stream, r], dev(x_=xp(r))).wait_recv()

    order = (1, 3, 2)
    for r in order:
        start(hx(0, r))
    for r in order:
        start(copy(ws.at[xp(r)], wa.at[t_id], wax_s.at[r], wax_r.at[r], dev(x_=xp(r))))

    def ya_pass(s, r):
        src = wa_ref = None
        xs = xm(r)
        up = wa.at[jnp.maximum(y - s, 0) * NX + xs]
        down = wa.at[jnp.minimum(y + s, NY - 1) * NX + xs]
        cu = copy(up, up, ya_s.at[0, s, r], ya_r.at[0, s, r], dev(y_=jnp.minimum(y + 1, NY - 1)))
        cd = copy(down, down, ya_s.at[1, s, r], ya_r.at[1, s, r], dev(y_=jnp.maximum(y - 1, 0)))
        return cu, cd

    def go_up(s):
        return jnp.logical_and(y < NY - 1, y >= s)

    def go_down(s):
        return jnp.logical_and(y > 0, y + s <= NY - 1)

    def send_ya(s, r):
        cu, cd = ya_pass(s, r)

        @pl.when(go_up(s))
        def _():
            cu.start()

        @pl.when(go_down(s))
        def _():
            cd.start()

    def wait_ya(s, r):
        xs = xm(r)
        lo = wa.at[jnp.maximum(y - s - 1, 0) * NX + xs]
        hi = wa.at[jnp.minimum(y + s + 1, NY - 1) * NX + xs]

        @pl.when(y >= s + 1)
        def _():
            copy(lo, lo, ya_s.at[0, s, r], ya_r.at[0, s, r], dev()).wait_recv()

        @pl.when(y + s + 1 <= NY - 1)
        def _():
            copy(hi, hi, ya_s.at[1, s, r], ya_r.at[1, s, r], dev()).wait_recv()

    def yb_pass(s):
        up = wb.at[pl.ds(jnp.maximum(y - s, 0) * NX, NX)]
        down = wb.at[pl.ds(jnp.minimum(y + s, NY - 1) * NX, NX)]
        cu = copy(up, up, yb_s.at[0, s], yb_r.at[0, s], dev(y_=jnp.minimum(y + 1, NY - 1)))
        cd = copy(down, down, yb_s.at[1, s], yb_r.at[1, s], dev(y_=jnp.maximum(y - 1, 0)))
        return cu, cd

    def send_yb(s):
        cu, cd = yb_pass(s)

        @pl.when(go_up(s))
        def _():
            cu.start()

        @pl.when(go_down(s))
        def _():
            cd.start()

    def wait_yb(s):
        lo = wb.at[pl.ds(jnp.maximum(y - s - 1, 0) * NX, NX)]
        hi = wb.at[pl.ds(jnp.minimum(y + s + 1, NY - 1) * NX, NX)]

        @pl.when(y >= s + 1)
        def _():
            copy(lo, lo, yb_s.at[0, s], yb_r.at[0, s], dev()).wait_recv()

        @pl.when(y + s + 1 <= NY - 1)
        def _():
            copy(hi, hi, yb_s.at[1, s], yb_r.at[1, s], dev()).wait_recv()

    def zblock(stream, b):
        return ht.at[:, yh if stream == 0 else 1 - yh, b, c]

    def send_c(stream, j, b):
        ref = zblock(stream, b)
        start(copy(ref, ref, c_s.at[stream, j], c_r.at[stream, j], dev(c_=1 - c)))

    def send_z(stream, k):
        up, down = lax.rem(z + NZ - k, NZ), lax.rem(z + k, NZ)
        if k < 4:
            ref = zblock(stream, up)
            start(copy(ref, ref, z_s.at[stream, 0, k], z_r.at[stream, 0, k], dev(z_=lax.rem(z + 1, NZ))))
        if k < 3:
            ref = zblock(stream, down)
            start(copy(ref, ref, z_s.at[stream, 1, k], z_r.at[stream, 1, k], dev(z_=lax.rem(z + NZ - 1, NZ))))
        send_c(stream, k, up)
        if 0 < k < 4:
            send_c(stream, 4 + k, down)

    def wait_z(stream, k):
        up, down = lax.rem(z + NZ - k - 1, NZ), lax.rem(z + k + 1, NZ)
        if k < 4:
            ref = zblock(stream, up)
            copy(ref, ref, z_s.at[stream, 0, k], z_r.at[stream, 0, k], dev()).wait_recv()
        if k < 3:
            ref = zblock(stream, down)
            copy(ref, ref, z_s.at[stream, 1, k], z_r.at[stream, 1, k], dev()).wait_recv()

    def wait_c(stream):
        for j in range(NZ):
            b = lax.rem(z + NZ - j, NZ) if j <= 4 else lax.rem(z + j - 4, NZ)
            ref = ht.at[:, yh if stream == 0 else 1 - yh, b, 1 - c]
            copy(ref, ref, c_s.at[stream, j], c_r.at[stream, j], dev()).wait_recv()

    def pa_copy(r, i):
        src = part_ref.at[pl.ds(i * RC, RC), pl.ds(pl.multiple_of(xp(r) * QA, SB), QA)]
        return copy(src, pa.at[x, pl.ds(i * RC, RC)], pa_s.at[r, i], pa_r.at[r, i], dev(x_=xp(r)))

    send_ya(0, 0)
    for r in order:
        start(copy(wb.at[t_id], wb.at[t_id], wbx_s.at[r], wbx_r.at[r], dev(x_=xp(r))))
    for r in order:
        start(copy(tg.at[x], tg.at[x], tg_s.at[r], tg_r.at[r], dev(x_=xp(r))))

    def wax_wait(r):
        ref = wa.at[y * NX + xm(r)]
        copy(ref, ref, wax_s.at[r], wax_r.at[r], dev()).wait_recv()

    for r in order:
        hx_wait(0, r)
    send_z(0, 0)
    other = ht.at[x, 1 - yh, z, c]
    copy(other, other, hy_s, hy_r, dev()).wait_recv()
    for r in order:
        start(hx(1, r))
    for i in range(NRC):
        for r in order:
            start(pa_copy(r, i))
    for r in order:
        wax_wait(r)
        send_ya(0, r)
    wait_ya(0, 0)
    send_ya(1, 0)
    wait_z(0, 0)
    send_z(0, 1)
    for r in order:
        hx_wait(1, r)
    send_z(1, 0)
    wait_ya(0, 1)
    send_ya(1, 1)
    wait_ya(1, 0)
    send_ya(2, 0)
    wait_z(0, 1)
    send_z(0, 2)
    wait_ya(0, 3)
    send_ya(1, 3)
    wait_z(1, 0)
    send_z(1, 1)
    wait_ya(0, 2)
    send_ya(1, 2)
    wait_ya(1, 1)
    send_ya(2, 1)
    wait_z(0, 2)
    send_z(0, 3)
    wait_ya(1, 3)
    send_ya(2, 3)
    wait_z(1, 1)
    send_z(1, 2)
    wait_ya(1, 2)
    send_ya(2, 2)
    for r in order:
        ref = wb.at[y * NX + xm(r)]
        copy(ref, ref, wbx_s.at[r], wbx_r.at[r], dev()).wait_recv()
    send_yb(0)
    wait_z(0, 3)
    send_c(0, 4, lax.rem(z + 4, NZ))
    wait_z(1, 2)
    send_z(1, 3)
    for r in order:
        ref = tg.at[xm(r)]
        copy(ref, ref, tg_s.at[r], tg_r.at[r], dev()).wait_recv()

    def spread(i, carry):
        row = tg[i].astype(jnp.float32)
        tt[i] = jnp.broadcast_to(row, (SB, ROWS)).T
        return carry

    lax.fori_loop(0, NX, spread, 0)
    wait_yb(0)
    send_yb(1)
    wait_z(1, 3)
    send_c(1, 4, lax.rem(z + 4, NZ))
    wait_c(0)
    wait_c(1)

    def turn(i, carry):
        for kb in range(8):
            blk = ht[i, kb // 4, (kb % 4) * 2:(kb % 4) * 2 + 2].reshape(SB, ROWS)
            hh[i, :, kb * SB:(kb + 1) * SB] = blk.T
        return carry

    lax.fori_loop(0, NX, turn, 0)
    for r in (0, 1, 3, 2):
        wait_ya(2, r)

    def stats(logits, base, tcol):
        width = logits.shape[1]
        top = jnp.max(logits, axis=1, keepdims=True)
        lse = top + jnp.log(jnp.sum(jnp.exp(logits - top), axis=1, keepdims=True))
        col = lax.broadcasted_iota(jnp.int32, logits.shape, 1).astype(jnp.float32)
        want = tcol - base.astype(jnp.float32)
        hit = col == jnp.concatenate([want] * (width // SB), axis=1)
        pick = jnp.sum(jnp.where(hit, logits, 0.0), axis=1, keepdims=True)
        lane = lax.broadcasted_iota(jnp.int32, (logits.shape[0], SB), 1)
        both = jnp.where(lane == 0, lse, jnp.where(lane == 1, pick, 0.0))
        return both.T[0:2]

    def do_a(xs, row):
        rows = pl.ds(row, RC)
        logits = jnp.dot(
            hh[xs, rows, :], wa[...].reshape(NX * NY * KLOC, QA), preferred_element_type=jnp.float32
        ) + pa[xs, rows, :].astype(jnp.float32)
        st[xs, :, rows] = stats(logits, v_id * VLOC + x * QA, tt[xs, rows, :])

    def do_b(row):
        rows = pl.ds(row, RC)
        logits = jnp.dot(
            hh[x, rows, :], wb[...].reshape(NX * NY * KLOC, BC), preferred_element_type=jnp.float32
        ) + pb[rows, :].astype(jnp.float32)
        stb[:, rows] = stats(logits, v_id * VLOC + 4 * QA, tt[x, rows, :])

    for d in own_pa:
        d.wait()
    own_pb.wait()

    def part(j, carry):
        k = jnp.maximum(j - NRC, 0)
        i = jnp.where(j < NRC, j, lax.div(k, 3))
        r = jnp.where(j < NRC, 0, 1 + lax.rem(2 * lax.rem(k, 3), 3))
        xs = lax.rem(x + NX - r, NX)
        row = pl.multiple_of(i * RC, RC)

        @pl.when(j >= NRC)
        def _():
            ref = pa.at[xs, pl.ds(row, RC)]
            copy(ref, ref, pa_s.at[r, i], pa_r.at[r, i], dev()).wait_recv()

        do_a(xs, row)
        return carry

    lax.fori_loop(0, NRC + 3, part, 0)
    wait_yb(1)
    send_yb(2)
    lax.fori_loop(NRC + 3, NRC + 3 * NRC, part, 0)

    for r in order:
        start(copy(st.at[xp(r)], sx.at[x], sx_s.at[r], sx_r.at[r], dev(x_=xp(r))))
    sx[x] = st[x]
    wait_yb(2)

    def part_b(i, carry):
        do_b(pl.multiple_of(i * RC, RC))
        return carry

    lax.fori_loop(0, NRC, part_b, 0)
    for r in order:
        ref = sx.at[xm(r)]
        copy(ref, ref, sx_s.at[r], sx_r.at[r], dev()).wait_recv()

    def merge(rows):
        lses, picks = [a[0:1] for a in rows], [a[1:2] for a in rows]
        top = functools.reduce(jnp.maximum, lses)
        total = sum(jnp.exp(a - top) for a in lses)
        return top + jnp.log(total), sum(picks)

    g = yh * 2 + c
    lse, pick = merge([sx[i] for i in range(NX)] + [stb[...]])
    sv[g, 0:1] = lse
    sv[g, 1:2] = pick
    for r in range(1, 4):
        to = dev(yh_=lax.rem(yh + r // 2, 2), c_=lax.rem(c + r % 2, 2))
        start(copy(sv.at[g], sv.at[g], sv_s.at[r], sv_r.at[r], to))
    for r in range(1, 4):
        ref = sv.at[lax.rem(yh + r // 2, 2) * 2 + lax.rem(c + r % 2, 2)]
        copy(ref, ref, sv_s.at[r], sv_r.at[r], dev()).wait_recv()
    lse, pick = merge([sv[i] for i in range(4)])
    sz[z, 0:1] = lse
    sz[z, 1:2] = pick
    for r in (4, 3, 5, 2, 6, 1, 7):
        start(copy(sz.at[z], sz.at[z], sz_s.at[r], sz_r.at[r], dev(z_=lax.rem(z + r, NZ))))
    for r in (1, 7, 2, 6, 3, 5, 4):
        ref = sz.at[lax.rem(z + NZ - r, NZ)]
        copy(ref, ref, sz_s.at[r], sz_r.at[r], dev()).wait_recv()
    lse, pick = merge([sz[i] for i in range(NZ)])
    out_ref[...] = lse - pick

    for d in sends:
        d.wait_send()
    for s in range(3):
        for r in range(NX):
            cu, cd = ya_pass(s, r)

            @pl.when(go_up(s))
            def _():
                cu.wait_send()

            @pl.when(go_down(s))
            def _():
                cd.wait_send()

        bu, bd = yb_pass(s)

        @pl.when(go_up(s))
        def _():
            bu.wait_send()

        @pl.when(go_down(s))
        def _():
            bd.wait_send()


def on_device(hidden, weight_values, scales, partial_logits, targets):
    vmem = pl.BlockSpec(memory_space=pltpu.VMEM)
    dma = pltpu.SemaphoreType.DMA
    bf, f32 = jnp.bfloat16, jnp.float32
    n = NX * NY
    loss = pl.pallas_call(
        kernel,
        out_shape=jax.ShapeDtypeStruct((1, ROWS), f32),
        in_specs=[vmem, vmem, vmem, pl.BlockSpec(memory_space=pl.ANY), vmem],
        out_specs=vmem,
        scratch_shapes=[
            pltpu.VMEM((NX, KLOC, QA), bf),
            pltpu.VMEM((n, KLOC, QA), bf),
            pltpu.VMEM((n, KLOC, BC), bf),
            pltpu.VMEM((NX, 2, NZ, 2, KSH, ROWS), bf),
            pltpu.VMEM((NX, ROWS, n * KLOC), bf),
            pltpu.VMEM((NX, ROWS, QA), bf),
            pltpu.VMEM((ROWS, BC), bf),
            pltpu.VMEM((NX, 1, ROWS), jnp.int32),
            pltpu.VMEM((NX, ROWS, SB), f32),
            pltpu.VMEM((NX, 2, ROWS), f32),
            pltpu.VMEM((2, ROWS), f32),
            pltpu.VMEM((NX, 2, ROWS), f32),
            pltpu.VMEM((4, 2, ROWS), f32),
            pltpu.VMEM((NZ, 2, ROWS), f32),
            dma, dma, dma((2, 4)), dma((2, 4)), dma((2, 2, 4)), dma((2, 2, 4)), dma((2, 8)), dma((2, 8)),
            dma((4,)), dma((4,)), dma((4,)), dma((4,)),
            dma((2, 3, 4)), dma((2, 3, 4)), dma((2, 3)), dma((2, 3)),
            dma((4, NRC)), dma((4, NRC)), dma((NRC,)), dma,
            dma((4,)), dma((4,)), dma((4,)), dma((4,)), dma((4,)), dma((4,)), dma((8,)), dma((8,)),
        ],
        compiler_params=pltpu.CompilerParams(
            collective_id=0, has_side_effects=True, vmem_limit_bytes=48 << 20
        ),
    )(hidden, weight_values, scales, partial_logits, targets.reshape(1, ROWS))
    return loss.reshape(ROWS)


def solution(mesh):
    in_specs = (P("tok", "voc"), P("tok", "voc"), P("tok", "voc"), P("tok", "voc"), P("tok"))
    return jax.shard_map(on_device, mesh=mesh, in_specs=in_specs, out_specs=P("tok"), check_vma=False)
```

time: 434 us -> 88.5 us (0.20)
  blocking collectives: 211 us -> 0 us
  waiting for transfers between devices: 154 us -> 0 us
  Pallas kernels: 0 us -> 82 us
  matrix products: 31.2 us -> 0 us
  between operations: 13.4 us -> 0.02 us
  local copies, waits for them, and re-layouts: 17.8 us -> 6.17 us
  other arithmetic: 6.47 us -> 0 us
    all_gather x2 -> x0, waiting for transfers between devices: 152 us -> none  [the longest x1 103 us: on_device(): lax.all_gather(weight_values, 'tok', axis=0, tiled=True)]
    psum x1 -> x0, blocking collectives: 89.8 us -> none  [on_device(): lax.psum((jnp.sum(jnp.exp(full - top[:, None]), axis=1), local_pick), 'voc')]
    pmax x1 -> x0, blocking collectives: 84.3 us -> none  [on_device(): top = lax.pmax(local_top, 'voc')]
    pallas_call x0 -> x1, Pallas kernels: none -> 82 us  [on_device(): pl.pallas_call(kernel, out_shape=jax.ShapeDtypeStruct((1, ROWS), f32), in...]
    all_gather x1 -> x0, blocking collectives: 37.1 us -> none  [on_device(): lax.all_gather(scales.astype(jnp.bfloat16), 'tok', axis=0, tiled=True)]
    dot_general x1 -> x0, matrix products: 31.2 us -> none  [on_device(): jnp.dot(wide, expand(lax.all_gather(weight_values, 'tok', axis=0, tiled=T...]
    mul x1 -> x0, local copies, waits for them, and re-layouts: 11.1 us -> none  [expand(): values.astype(jnp.float32).reshape(count, groups, width // groups)]
    reduce_sum x1 -> x0, other arithmetic: 5.15 us -> none  [on_device(): jnp.sum(jnp.exp(full - top[:, None]), axis=1)]
  transfers between devices with their start and end apart: 2 -> 0, of which waited for: 2 -> 0; matrix products, arithmetic and copies ran while one was open for 2% -> 0% of each run, Pallas kernels for 0% -> 0%
where the time goes in v1:
time: 88.5 us; the launch traced here: 88.2 us
  Pallas kernels  82 us (93%)
  local copies, waits for them, and re-layouts  6.17 us (7%)
    pallas_call x1, Pallas kernels, on_device(): pl.pallas_call(kernel, out_shape=jax.ShapeDtypeStruct((1, ROWS), f32), in...  82 us
    unnamed x9, local copies, waits for them, and re-layouts  6.17 us

profile of v1, /device:TPU:1, one launch (start us, length us, event | category | flops | bytes accessed | tf_op | source)
XLA Modules:
  0.0 88.2 jit_solution(943314432557838245)
XLA Ops:
  0.0 0.8 copy.7.sc_ref
  0.8 0.9 %copy.6.hid_ref = bf16[512,32]{1,0:T(8,128)(2,1)S(1)} copy(bf16[512,32]{0,1:T(8,128)(2,1)} %param.5) | data formatting | bytes 65536 | tf_op args[0]
  1.7 0.0 copy-start
  1.7 2.2 %copy-done = bf16[512,4096]{1,0:T(8,128)(2,1)S(1)} copy-done((bf16[512,4096]{1,0:T(8,128)(2,1)S(1)}, bf16[512,4096]{1,0:T(8,128)(2,1)}, u32[]{:S(2)}) %copy-start) | copy-done | bytes 4194328
  3.9 0.0 copy-start.1
  3.9 1.0 %copy-done.1 = bf16[64,4096]{1,0:T(8,128)(2,1)S(1)} copy-done((bf16[64,4096]{1,0:T(8,128)(2,1)S(1)}, bf16[64,4096]{1,0:T(8,128)(2,1)}, u32[]{:S(2)}) %copy-start.1) | copy-done | bytes 524312
  4.9 0.0 copy-start.2
  4.9 0.7 copy-done.2
  5.6 82.0 %shard_map.55 = f32[1,512]{1,0:T(1,128)S(1)} custom-call(bf16[512,32]{1,0:T(8,128)(2,1)S(1)} %copy.6.hid_ref, bf16[64,4096]{1,0:T(8,128)(2,1)S(1)} %copy-done.1, f32[64,32]{1,0:T(8,128)S(1)} %copy.7.sc_ref, bf16[512,4096]{1,0:T(8,128)(2,1)S(1)} %copy-done, s32[1,512]{1,0:T(1,128)S(1)} %bitcast.3), custom_call_target="tpu_custom_call" | custom-call | tf_op jit(solution)/shard_map/pallas_call | solution.py:438
  87.6 0.6 copy.9
Async XLA Ops:
  1.7 2.2 %copy-start = (bf16[512,4096]{1,0:T(8,128)(2,1)S(1)}, bf16[512,4096]{1,0:T(8,128)(2,1)}, u32[]{:S(2)}) copy-start(bf16[512,4096]{1,0:T(8,128)(2,1)} %part_ref.1) | copy-start | bytes 12582916
  3.9 1.0 %copy-start.1 = (bf16[64,4096]{1,0:T(8,128)(2,1)S(1)}, bf16[64,4096]{1,0:T(8,128)(2,1)}, u32[]{:S(2)}) copy-start(bf16[64,4096]{1,0:T(8,128)(2,1)} %w_ref.1) | copy-start | bytes 1572868
  4.9 0.7 copy-start.2

commit v2 on v1

--- a/solution.py
+++ b/solution.py
@@ -20,9 +20,9 @@
 
 def kernel(
     hid_ref, w_ref, sc_ref, part_ref, tgt_ref, out_ref,
-    ws, wa, wb, ht, hh, pa, pb, tg, tt, st, stb, sx, sv, sz,
+    wv, scv, ws, wa, wb, ht, hh, pa, pb, tg, tt, st, stb, sx, sv, in_l,
     hy_s, hy_r, hx_s, hx_r, z_s, z_r, c_s, c_r, wax_s, wax_r, wbx_s, wbx_r,
-    ya_s, ya_r, yb_s, yb_r, pa_s, pa_r, pa_l, pb_l, tg_s, tg_r, sx_s, sx_r, sv_s, sv_r, sz_s, sz_r,
+    ya_s, ya_r, yb_s, yb_r, pa_s, pa_r, pa_l, pb_l, tg_s, tg_r, sx_s, sx_r, sv_s, sv_r,
 ):
     t_id, v_id = lax.axis_index("tok"), lax.axis_index("voc")
     x, y = lax.rem(t_id, NX), lax.div(t_id, NX)
@@ -64,6 +64,14 @@
     def _():
         greet(dev(y_=y + 1))
 
+    loads = [
+        pltpu.make_async_copy(w_ref, wv, in_l.at[0]),
+        pltpu.make_async_copy(sc_ref, scv, in_l.at[1]),
+        pltpu.make_async_copy(hid_ref, ht.at[x, yh, z, c], in_l.at[2]),
+        pltpu.make_async_copy(tgt_ref, tg.at[x], in_l.at[3]),
+    ]
+    for d in loads:
+        d.start()
     own_pa = [
         pltpu.make_async_copy(
             part_ref.at[pl.ds(i * RC, RC), pl.ds(pl.multiple_of(x * QA, SB), QA)],
@@ -76,8 +84,12 @@
     own_pb = pltpu.make_async_copy(part_ref.at[:, pl.ds(4 * QA, BC)], pb, pb_l)
     own_pb.start()
 
+    for d in loads:
+        d.wait()
+    sc = scv[...].T
+
     def dense(g):
-        scaled = w_ref[:, g * SB:(g + 1) * SB].astype(jnp.float32) * sc_ref[:, g:g + 1]
+        scaled = wv[:, g * SB:(g + 1) * SB].astype(jnp.float32) * sc[:, g:g + 1]
         return scaled.astype(jnp.bfloat16)
 
     for q in range(NX):
@@ -86,13 +98,6 @@
     for g in range(BG):
         wb[t_id, :, g * SB:(g + 1) * SB] = dense(4 * QG + g)
     wa[t_id] = ws[x]
-    eye = (
-        lax.broadcasted_iota(jnp.int32, (KSH, KSH), 0) == lax.broadcasted_iota(jnp.int32, (KSH, KSH), 1)
-    ).astype(jnp.bfloat16)
-    ht[x, yh, z, c] = lax.dot_general(
-        eye, hid_ref[...], (((1,), (1,)), ((), ())), preferred_element_type=jnp.float32
-    ).astype(jnp.bfloat16)
-    tg[x] = tgt_ref[...]
 
     near = jnp.where(y > 0, 1, 0) + jnp.where(y < NY - 1, 1, 0)
     pl.semaphore_wait(bar, (NX - 1) + (NZ - 1) + 3 + near)
@@ -115,13 +120,8 @@
         copy(ref, ref, hx_s.at[stream, r], hx_r.at[stream, r], dev(x_=xp(r))).wait_recv()
 
     order = (1, 3, 2)
-    for r in order:
-        start(hx(0, r))
-    for r in order:
-        start(copy(ws.at[xp(r)], wa.at[t_id], wax_s.at[r], wax_r.at[r], dev(x_=xp(r))))
 
     def ya_pass(s, r):
-        src = wa_ref = None
         xs = xm(r)
         up = wa.at[jnp.maximum(y - s, 0) * NX + xs]
         down = wa.at[jnp.minimum(y + s, NY - 1) * NX + xs]
@@ -227,16 +227,26 @@
         src = part_ref.at[pl.ds(i * RC, RC), pl.ds(pl.multiple_of(xp(r) * QA, SB), QA)]
         return copy(src, pa.at[x, pl.ds(i * RC, RC)], pa_s.at[r, i], pa_r.at[r, i], dev(x_=xp(r)))
 
-    send_ya(0, 0)
-    for r in order:
-        start(copy(wb.at[t_id], wb.at[t_id], wbx_s.at[r], wbx_r.at[r], dev(x_=xp(r))))
-    for r in order:
-        start(copy(tg.at[x], tg.at[x], tg_s.at[r], tg_r.at[r], dev(x_=xp(r))))
-
     def wax_wait(r):
         ref = wa.at[y * NX + xm(r)]
         copy(ref, ref, wax_s.at[r], wax_r.at[r], dev()).wait_recv()
 
+    def turn(stream):
+        half = yh if stream == 0 else 1 - yh
+
+        def one(i, carry):
+            for kb in range(4):
+                blk = ht[i, half, kb * 2:kb * 2 + 2].reshape(SB, ROWS)
+                hh[i, :, pl.ds(pl.multiple_of(half * 4 * SB, SB) + kb * SB, SB)] = blk.T
+            return carry
+
+        lax.fori_loop(0, NX, one, 0)
+
+    for r in order:
+        start(hx(0, r))
+    send_ya(0, 0)
+    for r in order:
+        start(copy(ws.at[xp(r)], wa.at[t_id], wax_s.at[r], wax_r.at[r], dev(x_=xp(r))))
     for r in order:
         hx_wait(0, r)
     send_z(0, 0)
@@ -244,14 +254,21 @@
     copy(other, other, hy_s, hy_r, dev()).wait_recv()
     for r in order:
         start(hx(1, r))
+    for r in order:
+        start(copy(wb.at[t_id], wb.at[t_id], wbx_s.at[r], wbx_r.at[r], dev(x_=xp(r))))
+    for r in order:
+        start(copy(tg.at[x], tg.at[x], tg_s.at[r], tg_r.at[r], dev(x_=xp(r))))
     for i in range(NRC):
-        for r in order:
+        for r in (2, 1, 3):
             start(pa_copy(r, i))
-    for r in order:
-        wax_wait(r)
-        send_ya(0, r)
+    wax_wait(1)
+    send_ya(0, 1)
+    wax_wait(3)
+    send_ya(0, 3)
     wait_ya(0, 0)
     send_ya(1, 0)
+    wax_wait(2)
+    send_ya(0, 2)
     wait_z(0, 0)
     send_z(0, 1)
     for r in order:
@@ -263,20 +280,20 @@
     send_ya(2, 0)
     wait_z(0, 1)
     send_z(0, 2)
+    wait_z(1, 0)
+    send_z(1, 1)
     wait_ya(0, 3)
     send_ya(1, 3)
-    wait_z(1, 0)
-    send_z(1, 1)
+    wait_ya(1, 1)
+    send_ya(2, 1)
     wait_ya(0, 2)
     send_ya(1, 2)
-    wait_ya(1, 1)
-    send_ya(2, 1)
     wait_z(0, 2)
     send_z(0, 3)
+    wait_z(1, 1)
+    send_z(1, 2)
     wait_ya(1, 3)
     send_ya(2, 3)
-    wait_z(1, 1)
-    send_z(1, 2)
     wait_ya(1, 2)
     send_ya(2, 2)
     for r in order:
@@ -287,6 +304,7 @@
     send_c(0, 4, lax.rem(z + 4, NZ))
     wait_z(1, 2)
     send_z(1, 3)
+
     for r in order:
         ref = tg.at[xm(r)]
         copy(ref, ref, tg_s.at[r], tg_r.at[r], dev()).wait_recv()
@@ -297,20 +315,14 @@
         return carry
 
     lax.fori_loop(0, NX, spread, 0)
+    wait_c(0)
+    turn(0)
     wait_yb(0)
     send_yb(1)
     wait_z(1, 3)
     send_c(1, 4, lax.rem(z + 4, NZ))
-    wait_c(0)
     wait_c(1)
-
-    def turn(i, carry):
-        for kb in range(8):
-            blk = ht[i, kb // 4, (kb % 4) * 2:(kb % 4) * 2 + 2].reshape(SB, ROWS)
-            hh[i, :, kb * SB:(kb + 1) * SB] = blk.T
-        return carry
-
-    lax.fori_loop(0, NX, turn, 0)
+    turn(1)
     for r in (0, 1, 3, 2):
         wait_ya(2, r)
 
@@ -344,10 +356,14 @@
         d.wait()
     own_pb.wait()
 
+    def sx_copy(r):
+        to = lax.rem(x + NX - r, NX)
+        return copy(st.at[to], sx.at[x], sx_s.at[NX - r], sx_r.at[NX - r], dev(x_=to))
+
     def part(j, carry):
         k = jnp.maximum(j - NRC, 0)
         i = jnp.where(j < NRC, j, lax.div(k, 3))
-        r = jnp.where(j < NRC, 0, 1 + lax.rem(2 * lax.rem(k, 3), 3))
+        r = jnp.where(j < NRC, 0, 1 + lax.rem(lax.rem(k, 3) + 1, 3))
         xs = lax.rem(x + NX - r, NX)
         row = pl.multiple_of(i * RC, RC)
 
@@ -357,6 +373,11 @@
             copy(ref, ref, pa_s.at[r, i], pa_r.at[r, i], dev()).wait_recv()
 
         do_a(xs, row)
+
+        @pl.when(j >= NRC + 3 * (NRC - 1))
+        def _():
+            sx_copy(r).start()
+
         return carry
 
     lax.fori_loop(0, NRC + 3, part, 0)
@@ -364,8 +385,7 @@
     send_yb(2)
     lax.fori_loop(NRC + 3, NRC + 3 * NRC, part, 0)
 
-    for r in order:
-        start(copy(st.at[xp(r)], sx.at[x], sx_s.at[r], sx_r.at[r], dev(x_=xp(r))))
+    sends.extend(sx_copy(r) for r in order)
     sx[x] = st[x]
     wait_yb(2)
 
@@ -384,27 +404,19 @@
         total = sum(jnp.exp(a - top) for a in lses)
         return top + jnp.log(total), sum(picks)
 
-    g = yh * 2 + c
     lse, pick = merge([sx[i] for i in range(NX)] + [stb[...]])
-    sv[g, 0:1] = lse
-    sv[g, 1:2] = pick
-    for r in range(1, 4):
-        to = dev(yh_=lax.rem(yh + r // 2, 2), c_=lax.rem(c + r % 2, 2))
-        start(copy(sv.at[g], sv.at[g], sv_s.at[r], sv_r.at[r], to))
-    for r in range(1, 4):
-        ref = sv.at[lax.rem(yh + r // 2, 2) * 2 + lax.rem(c + r % 2, 2)]
-        copy(ref, ref, sv_s.at[r], sv_r.at[r], dev()).wait_recv()
-    lse, pick = merge([sv[i] for i in range(4)])
-    sz[z, 0:1] = lse
-    sz[z, 1:2] = pick
-    for r in (4, 3, 5, 2, 6, 1, 7):
-        start(copy(sz.at[z], sz.at[z], sz_s.at[r], sz_r.at[r], dev(z_=lax.rem(z + r, NZ))))
-    for r in (1, 7, 2, 6, 3, 5, 4):
-        ref = sz.at[lax.rem(z + NZ - r, NZ)]
-        copy(ref, ref, sz_s.at[r], sz_r.at[r], dev()).wait_recv()
-    lse, pick = merge([sz[i] for i in range(NZ)])
-    out_ref[...] = lse - pick
-
+    sv[v_id, 0:1] = lse
+    sv[v_id, 1:2] = pick
+
+    def peer(i, sign):
+        dz = (4, 3, 5, 2, 6, 1, 7, 0)[i // 4]
+        return (
+            lax.rem(yh + 1 - i % 4 // 2, 2), lax.rem(z + NZ + sign * dz, NZ), lax.rem(c + 1 - i % 2, 2)
+        )
+
+    for i in range(31):
+        to = peer(i, 1)
+        start(copy(sv.at[v_id], sv.at[v_id], sv_s.at[i], sv_r.at[i], dev(yh_=to[0], z_=to[1], c_=to[2])))
     for d in sends:
         d.wait_send()
     for s in range(3):
@@ -428,6 +440,15 @@
         @pl.when(go_down(s))
         def _():
             bd.wait_send()
+    for i in range(30, -1, -1):
+        a_, b_, c_ = peer(i, -1)
+        ref = sv.at[a_ * 16 + b_ * 2 + c_]
+        copy(ref, ref, sv_s.at[i], sv_r.at[i], dev()).wait_recv()
+    every = sv[...]
+    lses, picks = every[:, 0, :], every[:, 1, :]
+    top = jnp.max(lses, axis=0, keepdims=True)
+    total = jnp.sum(jnp.exp(lses - top), axis=0, keepdims=True)
+    out_ref[...] = top + jnp.log(total) - jnp.sum(picks, axis=0, keepdims=True)
 
 
 def on_device(hidden, weight_values, scales, partial_logits, targets):
@@ -438,9 +459,11 @@
     loss = pl.pallas_call(
         kernel,
         out_shape=jax.ShapeDtypeStruct((1, ROWS), f32),
-        in_specs=[vmem, vmem, vmem, pl.BlockSpec(memory_space=pl.ANY), vmem],
+        in_specs=[pl.BlockSpec(memory_space=pltpu.HBM)] * 5,
         out_specs=vmem,
         scratch_shapes=[
+            pltpu.VMEM((KLOC, VLOC), bf),
+            pltpu.VMEM((VLOC // SB, KLOC), f32),
             pltpu.VMEM((NX, KLOC, QA), bf),
             pltpu.VMEM((n, KLOC, QA), bf),
             pltpu.VMEM((n, KLOC, BC), bf),
@@ -453,18 +476,18 @@
             pltpu.VMEM((NX, 2, ROWS), f32),
             pltpu.VMEM((2, ROWS), f32),
             pltpu.VMEM((NX, 2, ROWS), f32),
-            pltpu.VMEM((4, 2, ROWS), f32),
-            pltpu.VMEM((NZ, 2, ROWS), f32),
+            pltpu.VMEM((32, 2, ROWS), f32),
+            dma((4,)),
             dma, dma, dma((2, 4)), dma((2, 4)), dma((2, 2, 4)), dma((2, 2, 4)), dma((2, 8)), dma((2, 8)),
             dma((4,)), dma((4,)), dma((4,)), dma((4,)),
             dma((2, 3, 4)), dma((2, 3, 4)), dma((2, 3)), dma((2, 3)),
             dma((4, NRC)), dma((4, NRC)), dma((NRC,)), dma,
-            dma((4,)), dma((4,)), dma((4,)), dma((4,)), dma((4,)), dma((4,)), dma((8,)), dma((8,)),
+            dma((4,)), dma((4,)), dma((4,)), dma((4,)), dma((31,)), dma((31,)),
         ],
         compiler_params=pltpu.CompilerParams(
-            collective_id=0, has_side_effects=True, vmem_limit_bytes=48 << 20
+            collective_id=0, has_side_effects=True, vmem_limit_bytes=60 << 20
         ),
-    )(hidden, weight_values, scales, partial_logits, targets.reshape(1, ROWS))
+    )(hidden.T, weight_values, scales.T, partial_logits, targets.reshape(1, ROWS))
     return loss.reshape(ROWS)
 
 

time: 88.5 us -> 82.6 us (0.933)
  local copies, waits for them, and re-layouts: 6.17 us -> 1.26 us
    unnamed x9 -> x1, local copies, waits for them, and re-layouts: 6.17 us -> 1.26 us
where the time goes in v2:
time: 82.6 us; the launch traced here: 82.5 us
  Pallas kernels  81.2 us (98%)
  local copies, waits for them, and re-layouts  1.26 us (2%)
    pallas_call x1, Pallas kernels, on_device(): pl.pallas_call(kernel, out_shape=jax.ShapeDtypeStruct((1, ROWS), f32), in...  81.2 us

profile of v2, /device:TPU:1, one launch (start us, length us, event | category | flops | bytes accessed | tf_op | source)
XLA Modules:
  0.0 82.5 jit_solution(2277183748700549126)
XLA Ops:
  0.0 81.2 %shard_map.55 = f32[1,512]{1,0:T(1,128)} custom-call(bf16[32,512]{1,0:T(8,128)(2,1)} %bitcast.4, bf16[64,4096]{1,0:T(8,128)(2,1)} %w_ref.1, f32[32,64]{1,0:T(8,128)} %bitcast.5, bf16[512,4096]{1,0:T(8,128)(2,1)} %part_ref.1, s32[1,512]{1,0:T(1,128)} %bitcast.7), custom_call_target="tpu_custom_call" | custom-call | tf_op jit(solution)/shard_map/pallas_call | solution.py:459
  81.2 1.3 %copy.7 = f32[512]{0:T(512)} copy(f32[512]{0:T(512)} %bitcast.6) | data formatting | bytes 4096

commit v3 on v2

--- a/solution.py
+++ b/solution.py
@@ -10,19 +10,20 @@
 MESH = pl.DeviceIdType.MESH
 NX, NY, NZ = 4, 4, 8
 ROWS, KLOC, VLOC, KSH, SB = 512, 64, 4096, 32, 128
-QG = 7
+QG = 6
 QA = QG * SB
-BC = VLOC - 4 * QA
-BG = BC // SB
+BG = VLOC // SB // NX - QG
+QB = BG * SB
+B0 = NX * QA
 RC = 256
 NRC = ROWS // RC
 
 
 def kernel(
     hid_ref, w_ref, sc_ref, part_ref, tgt_ref, out_ref,
-    wv, scv, ws, wa, wb, ht, hh, pa, pb, tg, tt, st, stb, sx, sv, in_l,
+    wv, scv, ws, wsb, wa, wb, ht, hh, pa, pb, pc, tg, tt, st, stb, sx, sv, in_l,
     hy_s, hy_r, hx_s, hx_r, z_s, z_r, c_s, c_r, wax_s, wax_r, wbx_s, wbx_r,
-    ya_s, ya_r, yb_s, yb_r, pa_s, pa_r, pa_l, pb_l, tg_s, tg_r, sx_s, sx_r, sv_s, sv_r,
+    ya_s, ya_r, yb_s, yb_r, pa_s, pa_r, pb_s, pb_r, pa_l, pb_l, tg_s, tg_r, sx_s, sx_r, sv_s, sv_r,
 ):
     t_id, v_id = lax.axis_index("tok"), lax.axis_index("voc")
     x, y = lax.rem(t_id, NX), lax.div(t_id, NX)
@@ -81,26 +82,19 @@
     ]
     for d in own_pa:
         d.start()
-    own_pb = pltpu.make_async_copy(part_ref.at[:, pl.ds(4 * QA, BC)], pb, pb_l)
-    own_pb.start()
-
-    for d in loads:
-        d.wait()
-    sc = scv[...].T
-
-    def dense(g):
-        scaled = wv[:, g * SB:(g + 1) * SB].astype(jnp.float32) * sc[:, g:g + 1]
-        return scaled.astype(jnp.bfloat16)
-
-    for q in range(NX):
-        for g in range(QG):
-            ws[q, :, g * SB:(g + 1) * SB] = dense(q * QG + g)
-    for g in range(BG):
-        wb[t_id, :, g * SB:(g + 1) * SB] = dense(4 * QG + g)
-    wa[t_id] = ws[x]
+    far = xp(2)
+    own_pb = [
+        pltpu.make_async_copy(
+            part_ref.at[:, pl.ds(pl.multiple_of(B0 + q * QB, SB), QB)], dst, pb_l.at[i]
+        )
+        for i, (q, dst) in enumerate(((x, pb.at[x]), (far, pc)))
+    ]
+    for d in own_pb:
+        d.start()
 
     near = jnp.where(y > 0, 1, 0) + jnp.where(y < NY - 1, 1, 0)
     pl.semaphore_wait(bar, (NX - 1) + (NZ - 1) + 3 + near)
+    loads[2].wait()
 
     sends = []
 
@@ -108,16 +102,13 @@
         d.start()
         sends.append(d)
 
-    hy = copy(ht.at[x, yh, z, c], ht.at[x, yh, z, c], hy_s, hy_r, dev(yh_=1 - yh))
-    start(hy)
-
-    def hx(stream, r):
-        ref = ht.at[x, yh if stream == 0 else 1 - yh, z, c]
-        return copy(ref, ref, hx_s.at[stream, r], hx_r.at[stream, r], dev(x_=xp(r)))
-
-    def hx_wait(stream, r):
-        ref = ht.at[xm(r), yh if stream == 0 else 1 - yh, z, c]
-        copy(ref, ref, hx_s.at[stream, r], hx_r.at[stream, r], dev(x_=xp(r))).wait_recv()
+    def hx(r):
+        ref = ht.at[x, yh, z, c]
+        return copy(ref, ref, hx_s.at[r], hx_r.at[r], dev(x_=xp(r)))
+
+    def hx_wait(r):
+        ref = ht.at[xm(r), yh, z, c]
+        copy(ref, ref, hx_s.at[r], hx_r.at[r], dev(x_=xp(r))).wait_recv()
 
     order = (1, 3, 2)
 
@@ -159,15 +150,15 @@
         def _():
             copy(hi, hi, ya_s.at[1, s, r], ya_r.at[1, s, r], dev()).wait_recv()
 
-    def yb_pass(s):
-        up = wb.at[pl.ds(jnp.maximum(y - s, 0) * NX, NX)]
-        down = wb.at[pl.ds(jnp.minimum(y + s, NY - 1) * NX, NX)]
-        cu = copy(up, up, yb_s.at[0, s], yb_r.at[0, s], dev(y_=jnp.minimum(y + 1, NY - 1)))
-        cd = copy(down, down, yb_s.at[1, s], yb_r.at[1, s], dev(y_=jnp.maximum(y - 1, 0)))
+    def yb_pass(p, s):
+        up = wb.at[p, pl.ds(jnp.maximum(y - s, 0) * NX, NX)]
+        down = wb.at[p, pl.ds(jnp.minimum(y + s, NY - 1) * NX, NX)]
+        cu = copy(up, up, yb_s.at[p, 0, s], yb_r.at[p, 0, s], dev(y_=jnp.minimum(y + 1, NY - 1)))
+        cd = copy(down, down, yb_s.at[p, 1, s], yb_r.at[p, 1, s], dev(y_=jnp.maximum(y - 1, 0)))
         return cu, cd
 
-    def send_yb(s):
-        cu, cd = yb_pass(s)
+    def send_yb(p, s):
+        cu, cd = yb_pass(p, s)
 
         @pl.when(go_up(s))
         def _():
@@ -177,20 +168,27 @@
         def _():
             cd.start()
 
-    def wait_yb(s):
-        lo = wb.at[pl.ds(jnp.maximum(y - s - 1, 0) * NX, NX)]
-        hi = wb.at[pl.ds(jnp.minimum(y + s + 1, NY - 1) * NX, NX)]
+    def wait_yb(p, s):
+        lo = wb.at[p, pl.ds(jnp.maximum(y - s - 1, 0) * NX, NX)]
+        hi = wb.at[p, pl.ds(jnp.minimum(y + s + 1, NY - 1) * NX, NX)]
 
         @pl.when(y >= s + 1)
         def _():
-            copy(lo, lo, yb_s.at[0, s], yb_r.at[0, s], dev()).wait_recv()
+            copy(lo, lo, yb_s.at[p, 0, s], yb_r.at[p, 0, s], dev()).wait_recv()
 
         @pl.when(y + s + 1 <= NY - 1)
         def _():
-            copy(hi, hi, yb_s.at[1, s], yb_r.at[1, s], dev()).wait_recv()
+            copy(hi, hi, yb_s.at[p, 1, s], yb_r.at[p, 1, s], dev()).wait_recv()
 
     def zblock(stream, b):
         return ht.at[:, yh if stream == 0 else 1 - yh, b, c]
+
+    def zhalf(stream, h, b):
+        return ht.at[2 * h:2 * h + 2, yh if stream == 0 else 1 - yh, b, c]
+
+    def zcopy(stream, h, way, k, b, to):
+        ref = zhalf(stream, h, b)
+        return copy(ref, ref, z_s.at[stream, h, way, k], z_r.at[stream, h, way, k], to)
 
     def send_c(stream, j, b):
         ref = zblock(stream, b)
@@ -198,24 +196,26 @@
 
     def send_z(stream, k):
         up, down = lax.rem(z + NZ - k, NZ), lax.rem(z + k, NZ)
-        if k < 4:
-            ref = zblock(stream, up)
-            start(copy(ref, ref, z_s.at[stream, 0, k], z_r.at[stream, 0, k], dev(z_=lax.rem(z + 1, NZ))))
-        if k < 3:
-            ref = zblock(stream, down)
-            start(copy(ref, ref, z_s.at[stream, 1, k], z_r.at[stream, 1, k], dev(z_=lax.rem(z + NZ - 1, NZ))))
+        for h in range(2):
+            if k < 4 - h:
+                start(zcopy(stream, h, 0, k, up, dev(z_=lax.rem(z + 1, NZ))))
+            if k < 3 + h:
+                start(zcopy(stream, h, 1, k, down, dev(z_=lax.rem(z + NZ - 1, NZ))))
         send_c(stream, k, up)
         if 0 < k < 4:
             send_c(stream, 4 + k, down)
 
-    def wait_z(stream, k):
+    def step_z(stream, k):
         up, down = lax.rem(z + NZ - k - 1, NZ), lax.rem(z + k + 1, NZ)
-        if k < 4:
-            ref = zblock(stream, up)
-            copy(ref, ref, z_s.at[stream, 0, k], z_r.at[stream, 0, k], dev()).wait_recv()
+        for h in range(2):
+            if k < 4 - h:
+                zcopy(stream, h, 0, k, up, dev()).wait_recv()
+            if k < 3 + h:
+                zcopy(stream, h, 1, k, down, dev()).wait_recv()
         if k < 3:
-            ref = zblock(stream, down)
-            copy(ref, ref, z_s.at[stream, 1, k], z_r.at[stream, 1, k], dev()).wait_recv()
+            send_z(stream, k + 1)
+        else:
+            send_c(stream, 4, up)
 
     def wait_c(stream):
         for j in range(NZ):
@@ -227,6 +227,15 @@
         src = part_ref.at[pl.ds(i * RC, RC), pl.ds(pl.multiple_of(xp(r) * QA, SB), QA)]
         return copy(src, pa.at[x, pl.ds(i * RC, RC)], pa_s.at[r, i], pa_r.at[r, i], dev(x_=xp(r)))
 
+    def pb_copy(r, i):
+        src = part_ref.at[pl.ds(i * RC, RC), pl.ds(pl.multiple_of(B0 + xp(r) * QB, SB), QB)]
+        return copy(src, pb.at[x, pl.ds(i * RC, RC)], pb_s.at[r, i], pb_r.at[r, i], dev(x_=xp(r)))
+
+    def wbx_wait(p):
+        for r in order:
+            ref = wb.at[p, y * NX + xm(r)]
+            copy(ref, ref, wbx_s.at[p, r], wbx_r.at[p, r], dev()).wait_recv()
+
     def wax_wait(r):
         ref = wa.at[y * NX + xm(r)]
         copy(ref, ref, wax_s.at[r], wax_r.at[r], dev()).wait_recv()
@@ -242,68 +251,85 @@
 
         lax.fori_loop(0, NX, one, 0)
 
+    def send_wb(p):
+        for r in order:
+            start(copy(wsb.at[xp(r + 2 * p)], wb.at[p, t_id], wbx_s.at[p, r], wbx_r.at[p, r], dev(x_=xp(r))))
+
+    def pass_ya(s, r):
+        wait_ya(s - 1, r)
+        send_ya(s, r)
+
+    def pass_yb(p, s):
+        wait_yb(p, s - 1)
+        send_yb(p, s)
+
     for r in order:
-        start(hx(0, r))
+        start(hx(r))
+
+    for i in (0, 1, 3):
+        loads[i].wait()
+    sc = scv[...].T
+
+    def dense(g):
+        scaled = wv[:, g * SB:(g + 1) * SB].astype(jnp.float32) * sc[:, g:g + 1]
+        return scaled.astype(jnp.bfloat16)
+
+    for q in range(NX):
+        for g in range(QG):
+            ws[q, :, g * SB:(g + 1) * SB] = dense(q * QG + g)
+        for g in range(BG):
+            wsb[q, :, g * SB:(g + 1) * SB] = dense(NX * QG + q * BG + g)
+    wa[t_id] = ws[x]
+    wb[0, t_id] = wsb[x]
+    wb[1, t_id] = wsb[far]
+
     send_ya(0, 0)
     for r in order:
         start(copy(ws.at[xp(r)], wa.at[t_id], wax_s.at[r], wax_r.at[r], dev(x_=xp(r))))
-    for r in order:
-        hx_wait(0, r)
-    send_z(0, 0)
-    other = ht.at[x, 1 - yh, z, c]
-    copy(other, other, hy_s, hy_r, dev()).wait_recv()
-    for r in order:
-        start(hx(1, r))
-    for r in order:
-        start(copy(wb.at[t_id], wb.at[t_id], wbx_s.at[r], wbx_r.at[r], dev(x_=xp(r))))
+    send_wb(0)
+    send_wb(1)
     for r in order:
         start(copy(tg.at[x], tg.at[x], tg_s.at[r], tg_r.at[r], dev(x_=xp(r))))
     for i in range(NRC):
         for r in (2, 1, 3):
             start(pa_copy(r, i))
+    for i in range(NRC):
+        for r in (1, 3):
+            start(pb_copy(r, i))
+    for r in order:
+        hx_wait(r)
+    send_z(0, 0)
+    ref = zblock(0, z)
+    start(copy(ref, ref, hy_s, hy_r, dev(yh_=1 - yh)))
     wax_wait(1)
     send_ya(0, 1)
     wax_wait(3)
     send_ya(0, 3)
-    wait_ya(0, 0)
-    send_ya(1, 0)
+    pass_ya(1, 0)
     wax_wait(2)
     send_ya(0, 2)
-    wait_z(0, 0)
-    send_z(0, 1)
-    for r in order:
-        hx_wait(1, r)
+    step_z(0, 0)
+    ref = zblock(1, z)
+    copy(ref, ref, hy_s, hy_r, dev()).wait_recv()
     send_z(1, 0)
-    wait_ya(0, 1)
-    send_ya(1, 1)
-    wait_ya(1, 0)
-    send_ya(2, 0)
-    wait_z(0, 1)
-    send_z(0, 2)
-    wait_z(1, 0)
-    send_z(1, 1)
-    wait_ya(0, 3)
-    send_ya(1, 3)
-    wait_ya(1, 1)
-    send_ya(2, 1)
-    wait_ya(0, 2)
-    send_ya(1, 2)
-    wait_z(0, 2)
-    send_z(0, 3)
-    wait_z(1, 1)
-    send_z(1, 2)
-    wait_ya(1, 3)
-    send_ya(2, 3)
-    wait_ya(1, 2)
-    send_ya(2, 2)
-    for r in order:
-        ref = wb.at[y * NX + xm(r)]
-        copy(ref, ref, wbx_s.at[r], wbx_r.at[r], dev()).wait_recv()
-    send_yb(0)
-    wait_z(0, 3)
-    send_c(0, 4, lax.rem(z + 4, NZ))
-    wait_z(1, 2)
-    send_z(1, 3)
+    pass_ya(1, 1)
+    pass_ya(2, 0)
+    pass_ya(1, 3)
+    pass_ya(1, 2)
+    step_z(0, 1)
+    wbx_wait(0)
+    send_yb(0, 0)
+    step_z(1, 0)
+    pass_ya(2, 1)
+    pass_ya(2, 3)
+    step_z(0, 2)
+    pass_ya(2, 2)
+    step_z(1, 1)
+    wbx_wait(1)
+    send_yb(1, 0)
+    step_z(0, 3)
+    step_z(1, 2)
+    pass_yb(0, 1)
 
     for r in order:
         ref = tg.at[xm(r)]
@@ -317,10 +343,8 @@
     lax.fori_loop(0, NX, spread, 0)
     wait_c(0)
     turn(0)
-    wait_yb(0)
-    send_yb(1)
-    wait_z(1, 3)
-    send_c(1, 4, lax.rem(z + 4, NZ))
+    step_z(1, 3)
+    pass_yb(1, 1)
     wait_c(1)
     turn(1)
     for r in (0, 1, 3, 2):
@@ -343,18 +367,19 @@
         logits = jnp.dot(
             hh[xs, rows, :], wa[...].reshape(NX * NY * KLOC, QA), preferred_element_type=jnp.float32
         ) + pa[xs, rows, :].astype(jnp.float32)
-        st[xs, :, rows] = stats(logits, v_id * VLOC + x * QA, tt[xs, rows, :])
-
-    def do_b(row):
+        st[xs, 0:2, rows] = stats(logits, v_id * VLOC + x * QA, tt[xs, rows, :])
+
+    def do_b(p, xs, row, partial):
         rows = pl.ds(row, RC)
         logits = jnp.dot(
-            hh[x, rows, :], wb[...].reshape(NX * NY * KLOC, BC), preferred_element_type=jnp.float32
-        ) + pb[rows, :].astype(jnp.float32)
-        stb[:, rows] = stats(logits, v_id * VLOC + 4 * QA, tt[x, rows, :])
-
-    for d in own_pa:
+            hh[xs, rows, :], wb[p].reshape(NX * NY * KLOC, QB), preferred_element_type=jnp.float32
+        ) + partial.astype(jnp.float32)
+        return stats(logits, v_id * VLOC + B0 + xp(2 * p) * QB, tt[xs, rows, :])
+
+    for d in own_pa + own_pb:
         d.wait()
-    own_pb.wait()
+    none = lax.broadcasted_iota(jnp.int32, (2, ROWS), 0) == 0
+    st[far, 2:4] = jnp.where(none, -1e30, 0.0)
 
     def sx_copy(r):
         to = lax.rem(x + NX - r, NX)
@@ -374,37 +399,85 @@
 
         do_a(xs, row)
 
-        @pl.when(j >= NRC + 3 * (NRC - 1))
+        @pl.when(j == NRC + 3 * (NRC - 1))
+        def _():
+            sx_copy(2).start()
+
+        return carry
+
+    def part_b(j, carry):
+        k = jnp.maximum(j - NRC, 0)
+        i = jnp.where(j < NRC, j, lax.div(k, 2))
+        r = jnp.where(j < NRC, 0, 1 + 2 * lax.rem(k, 2))
+        xs = lax.rem(x + NX - r, NX)
+        row = pl.multiple_of(i * RC, RC)
+
+        @pl.when(j >= NRC)
+        def _():
+            ref = pb.at[xs, pl.ds(row, RC)]
+            copy(ref, ref, pb_s.at[r, i], pb_r.at[r, i], dev()).wait_recv()
+
+        st[xs, 2:4, pl.ds(row, RC)] = do_b(0, xs, row, pb[xs, pl.ds(row, RC), :])
+
+        @pl.when(j >= NRC + 2 * (NRC - 1))
         def _():
             sx_copy(r).start()
 
         return carry
 
-    lax.fori_loop(0, NRC + 3, part, 0)
-    wait_yb(1)
-    send_yb(2)
+    def part_c(i, carry):
+        row = pl.multiple_of(i * RC, RC)
+        stb[:, pl.ds(row, RC)] = do_b(1, x, row, pc[pl.ds(row, RC), :])
+        return carry
+
+    lax.fori_loop(0, NRC, part, 0)
+    pass_yb(0, 2)
+    lax.fori_loop(NRC, NRC + 3, part, 0)
+    pass_yb(1, 2)
     lax.fori_loop(NRC + 3, NRC + 3 * NRC, part, 0)
-
+    wait_yb(0, 2)
+    lax.fori_loop(0, NRC + 2 * NRC, part_b, 0)
+    n_early = len(sends)
     sends.extend(sx_copy(r) for r in order)
     sx[x] = st[x]
-    wait_yb(2)
-
-    def part_b(i, carry):
-        do_b(pl.multiple_of(i * RC, RC))
-        return carry
-
-    lax.fori_loop(0, NRC, part_b, 0)
+    wait_yb(1, 2)
+    lax.fori_loop(0, NRC, part_c, 0)
+    for d in sends[:n_early]:
+        d.wait_send()
+    for s in range(3):
+        for r in range(NX):
+            cu, cd = ya_pass(s, r)
+
+            @pl.when(go_up(s))
+            def _():
+                cu.wait_send()
+
+            @pl.when(go_down(s))
+            def _():
+                cd.wait_send()
+
+        for p in range(2):
+            bu, bd = yb_pass(p, s)
+
+            @pl.when(go_up(s))
+            def _():
+                bu.wait_send()
+
+            @pl.when(go_down(s))
+            def _():
+                bd.wait_send()
+
     for r in order:
         ref = sx.at[xm(r)]
         copy(ref, ref, sx_s.at[r], sx_r.at[r], dev()).wait_recv()
 
-    def merge(rows):
-        lses, picks = [a[0:1] for a in rows], [a[1:2] for a in rows]
-        top = functools.reduce(jnp.maximum, lses)
-        total = sum(jnp.exp(a - top) for a in lses)
-        return top + jnp.log(total), sum(picks)
-
-    lse, pick = merge([sx[i] for i in range(NX)] + [stb[...]])
+    mine = sx[...]
+    extra = stb[...]
+    lses = jnp.concatenate([mine[:, 0, :], mine[:, 2, :]], axis=0)
+    top = jnp.maximum(jnp.max(lses, axis=0, keepdims=True), extra[0:1])
+    total = jnp.sum(jnp.exp(lses - top), axis=0, keepdims=True) + jnp.exp(extra[0:1] - top)
+    lse = top + jnp.log(total)
+    pick = jnp.sum(mine[:, 1, :] + mine[:, 3, :], axis=0, keepdims=True) + extra[1:2]
     sv[v_id, 0:1] = lse
     sv[v_id, 1:2] = pick
 
@@ -417,29 +490,8 @@
     for i in range(31):
         to = peer(i, 1)
         start(copy(sv.at[v_id], sv.at[v_id], sv_s.at[i], sv_r.at[i], dev(yh_=to[0], z_=to[1], c_=to[2])))
-    for d in sends:
+    for d in sends[n_early:]:
         d.wait_send()
-    for s in range(3):
-        for r in range(NX):
-            cu, cd = ya_pass(s, r)
-
-            @pl.when(go_up(s))
-            def _():
-                cu.wait_send()
-
-            @pl.when(go_down(s))
-            def _():
-                cd.wait_send()
-
-        bu, bd = yb_pass(s)
-
-        @pl.when(go_up(s))
-        def _():
-            bu.wait_send()
-
-        @pl.when(go_down(s))
-        def _():
-            bd.wait_send()
     for i in range(30, -1, -1):
         a_, b_, c_ = peer(i, -1)
         ref = sv.at[a_ * 16 + b_ * 2 + c_]
@@ -465,23 +517,25 @@
             pltpu.VMEM((KLOC, VLOC), bf),
             pltpu.VMEM((VLOC // SB, KLOC), f32),
             pltpu.VMEM((NX, KLOC, QA), bf),
+            pltpu.VMEM((NX, KLOC, QB), bf),
             pltpu.VMEM((n, KLOC, QA), bf),
-            pltpu.VMEM((n, KLOC, BC), bf),
+            pltpu.VMEM((2, n, KLOC, QB), bf),
             pltpu.VMEM((NX, 2, NZ, 2, KSH, ROWS), bf),
             pltpu.VMEM((NX, ROWS, n * KLOC), bf),
             pltpu.VMEM((NX, ROWS, QA), bf),
-            pltpu.VMEM((ROWS, BC), bf),
+            pltpu.VMEM((NX, ROWS, QB), bf),
+            pltpu.VMEM((ROWS, QB), bf),
             pltpu.VMEM((NX, 1, ROWS), jnp.int32),
             pltpu.VMEM((NX, ROWS, SB), f32),
-            pltpu.VMEM((NX, 2, ROWS), f32),
+            pltpu.VMEM((NX, 4, ROWS), f32),
             pltpu.VMEM((2, ROWS), f32),
-            pltpu.VMEM((NX, 2, ROWS), f32),
+            pltpu.VMEM((NX, 4, ROWS), f32),
             pltpu.VMEM((32, 2, ROWS), f32),
             dma((4,)),
-            dma, dma, dma((2, 4)), dma((2, 4)), dma((2, 2, 4)), dma((2, 2, 4)), dma((2, 8)), dma((2, 8)),
-            dma((4,)), dma((4,)), dma((4,)), dma((4,)),
-            dma((2, 3, 4)), dma((2, 3, 4)), dma((2, 3)), dma((2, 3)),
-            dma((4, NRC)), dma((4, NRC)), dma((NRC,)), dma,
+            dma, dma, dma((4,)), dma((4,)), dma((2, 2, 2, 4)), dma((2, 2, 2, 4)), dma((2, 8)), dma((2, 8)),
+            dma((4,)), dma((4,)), dma((2, 4)), dma((2, 4)),
+            dma((2, 3, 4)), dma((2, 3, 4)), dma((2, 2, 3)), dma((2, 2, 3)),
+            dma((4, NRC)), dma((4, NRC)), dma((4, NRC)), dma((4, NRC)), dma((NRC,)), dma((2,)),
             dma((4,)), dma((4,)), dma((4,)), dma((4,)), dma((31,)), dma((31,)),
         ],
         compiler_params=pltpu.CompilerParams(

time: 82.6 us -> 81.9 us (level)
  no operation moved by 1% of the time
where the time goes in v3:
time: 81.9 us; the launch traced here: 81.8 us
  Pallas kernels  80.5 us (98%)
  local copies, waits for them, and re-layouts  1.26 us (2%)
    pallas_call x1, Pallas kernels, on_device(): pl.pallas_call(kernel, out_shape=jax.ShapeDtypeStruct((1, ROWS), f32), in...  80.5 us

profile of v3, /device:TPU:1, one launch (start us, length us, event | category | flops | bytes accessed | tf_op | source)
XLA Modules:
  0.0 81.8 jit_solution(15970850874564535937)
XLA Ops:
  0.0 80.5 %shard_map.55 = f32[1,512]{1,0:T(1,128)} custom-call(bf16[32,512]{1,0:T(8,128)(2,1)} %bitcast.4, bf16[64,4096]{1,0:T(8,128)(2,1)} %w_ref.1, f32[32,64]{1,0:T(8,128)} %bitcast.5, bf16[512,4096]{1,0:T(8,128)(2,1)} %part_ref.1, s32[1,512]{1,0:T(1,128)} %bitcast.7), custom_call_target="tpu_custom_call" | custom-call | tf_op jit(solution)/shard_map/pallas_call | solution.py:511
  80.5 1.3 %copy.7 = f32[512]{0:T(512)} copy(f32[512]{0:T(512)} %bitcast.6) | data formatting | bytes 4096

commit v4 on v3

--- a/solution.py
+++ b/solution.py
@@ -406,20 +406,20 @@
         return carry
 
     def part_b(j, carry):
-        k = jnp.maximum(j - NRC, 0)
-        i = jnp.where(j < NRC, j, lax.div(k, 2))
-        r = jnp.where(j < NRC, 0, 1 + 2 * lax.rem(k, 2))
+        own = j >= 2 * NRC
+        i = jnp.where(own, j - 2 * NRC, lax.div(j, 2))
+        r = jnp.where(own, 0, 1 + 2 * lax.rem(j, 2))
         xs = lax.rem(x + NX - r, NX)
         row = pl.multiple_of(i * RC, RC)
 
-        @pl.when(j >= NRC)
+        @pl.when(j < 2 * NRC)
         def _():
             ref = pb.at[xs, pl.ds(row, RC)]
             copy(ref, ref, pb_s.at[r, i], pb_r.at[r, i], dev()).wait_recv()
 
         st[xs, 2:4, pl.ds(row, RC)] = do_b(0, xs, row, pb[xs, pl.ds(row, RC), :])
 
-        @pl.when(j >= NRC + 2 * (NRC - 1))
+        @pl.when(jnp.logical_and(j >= 2 * (NRC - 1), j < 2 * NRC))
         def _():
             sx_copy(r).start()
 

time: 81.9 us -> 81.4 us (level)
  no operation moved by 1% of the time
where the time goes in v4:
time: 81.4 us; the launch traced here: 81.3 us
  Pallas kernels  80 us (98%)
  local copies, waits for them, and re-layouts  1.26 us (2%)
    pallas_call x1, Pallas kernels, on_device(): pl.pallas_call(kernel, out_shape=jax.ShapeDtypeStruct((1, ROWS), f32), in...  80 us

profile of v4, /device:TPU:1, one launch (start us, length us, event | category | flops | bytes accessed | tf_op | source)
XLA Modules:
  0.0 81.3 jit_solution(17947376769049151597)
XLA Ops:
  0.0 80.0 %shard_map.55 = f32[1,512]{1,0:T(1,128)} custom-call(bf16[32,512]{1,0:T(8,128)(2,1)} %bitcast.4, bf16[64,4096]{1,0:T(8,128)(2,1)} %w_ref.1, f32[32,64]{1,0:T(8,128)} %bitcast.5, bf16[512,4096]{1,0:T(8,128)(2,1)} %part_ref.1, s32[1,512]{1,0:T(1,128)} %bitcast.7), custom_call_target="tpu_custom_call" | custom-call | tf_op jit(solution)/shard_map/pallas_call | solution.py:511
  80.0 1.3 %copy.7 = f32[512]{0:T(512)} copy(f32[512]{0:T(512)} %bitcast.6) | data formatting | bytes 4096
